TPU v7x, 512 devices: a whole 4x8x8 slice. The times are simulated.
512 devices in a mesh: phase: 8 (over z), ctx: 64 (over x, y, core).
Axes of the slice: x: 4, y: 8, z: 8, core: 2. Of those that a mesh axis runs over, the one named last changes fastest.
Arguments:
- activations: bfloat16 [8, 8192, 4096], P('phase', 'ctx'), may hold values from -6 to 6
- norm_gain: bfloat16 [8, 4096], P('phase'), may hold values from 0.25 to 1.75
- short_taps: bfloat16 [8, 3, 3, 4096], P('phase'), may hold values from -3 to 3
- skip_gain: bfloat16 [8, 4096], P('phase'), may hold values from 0.19921875 to 1.5
- time_const: float32 [8, 4096, 16], P('phase', 'ctx'), may hold values from 25 to 32768
- residues: float32 [8, 4096, 16], P('phase', 'ctx'), may hold values from -2 to 2
Outputs:
- handed: bfloat16 [8, 8192, 4096], P('phase', 'ctx')
All inputs are finite; a program needn't handle non-finite values.
Results may differ from a plain program's by a relative error of at most 0.0058.
Values may be sent and summed in bfloat16 or wider, within the bound.
A program may use at most 128 MiB of HBM per device.

v0:
```python
import math
import jax
import jax.numpy as jnp
from jax import lax
from jax.sharding import PartitionSpec as P

HIGHEST_PRECISION = lax.Precision.HIGHEST


def from_behind(shard, axis, by):
    count = lax.axis_size(axis)
    pairs = [(i, i + by) for i in range(count) if 0 <= i + by < count]
    return lax.ppermute(shard, axis, pairs)


def from_behind_2(block, axis, distance):
    devices = range(lax.axis_size(axis))
    route = [((i - distance) % len(devices), i) for i in devices]
    return lax.ppermute(block, axis, route)


def circle_angle(product, modulus):
    return 2.0 * math.pi / modulus * (product % modulus).astype(jnp.float32)


def filter_spectrum(decay_time, residue, frequency, padded_length, length):
    theta = circle_angle(frequency, padded_length)
    half_sine = jnp.sin(0.5 * theta)[None]
    full_sine = jnp.sin(theta)[None]
    parity = (1 - 2 * (frequency % 2)).astype(jnp.float32)[None]
    shape = (decay_time.shape[0],) + frequency.shape
    real_part = jnp.zeros(shape, jnp.float32)
    imag_part = jnp.zeros(shape, jnp.float32)
    for mode in range(decay_time.shape[1]):
        decay_rate = 1.0 / decay_time[:, mode][:, None, None]
        damping = jnp.exp(-decay_rate)
        leftover = -jnp.expm1(-decay_rate)
        weight = residue[:, mode][:, None, None] * jnp.sqrt(-jnp.expm1(-2.0 * decay_rate))
        numerator = weight * (1.0 - jnp.exp(-decay_rate * length) * parity)
        denom_real = leftover + 2.0 * damping * half_sine * half_sine
        denom_imag = damping * full_sine
        magnitude = denom_real * denom_real + denom_imag * denom_imag
        real_part = real_part + numerator * denom_real / magnitude
        imag_part = imag_part - numerator * denom_imag / magnitude
    return (real_part, imag_part)


def spectral_conv(mixed_in, decay_time, residue):
    devices = lax.axis_size("ctx")
    length, channels = mixed_in.shape
    local_channels = channels // devices
    sequence = length * devices
    pieces = jnp.transpose(mixed_in).reshape(devices, local_channels, length)
    lines = lax.all_to_all(pieces, "ctx", split_axis=0, concat_axis=2, tiled=True)[0]
    col_count = 128
    padded_length = 2 * sequence
    row_count = padded_length // col_count
    used_rows = row_count // 2
    row_index = jnp.arange(row_count, dtype=jnp.int32)
    used_index = jnp.arange(used_rows, dtype=jnp.int32)
    col_index = jnp.arange(col_count, dtype=jnp.int32)
    row_angle = circle_angle(row_index[:, None] * used_index[None, :], row_count)
    cos_rows = jnp.cos(row_angle)
    sin_rows = jnp.sin(row_angle)
    turn_angle = circle_angle(row_index[:, None] * col_index[None, :], padded_length)
    cos_turn = jnp.cos(turn_angle)
    sin_turn = jnp.sin(turn_angle)
    col_angle = circle_angle(col_index[:, None] * col_index[None, :], col_count)
    cos_cols = jnp.cos(col_angle)
    sin_cols = jnp.sin(col_angle)
    frequency = row_index[:, None] + row_count * col_index[None, :]
    group_size = math.gcd(local_channels, 16)
    group_count = local_channels // group_size
    mode_count = decay_time.shape[1]

    def one_group(parts):
        signal_part, time_part, residue_part = parts
        signal = signal_part.astype(jnp.float32)
        first_real = jnp.einsum("ka,cab->ckb", cos_rows, signal, precision=HIGHEST_PRECISION)
        first_imag = -jnp.einsum("ka,cab->ckb", sin_rows, signal, precision=HIGHEST_PRECISION)
        turned_real = first_real * cos_turn + first_imag * sin_turn
        turned_imag = first_imag * cos_turn - first_real * sin_turn
        freq_real = jnp.einsum(
            "ckb,bq->ckq", turned_real, cos_cols, precision=HIGHEST_PRECISION
        ) + jnp.einsum("ckb,bq->ckq", turned_imag, sin_cols, precision=HIGHEST_PRECISION)
        freq_imag = jnp.einsum(
            "ckb,bq->ckq", turned_imag, cos_cols, precision=HIGHEST_PRECISION
        ) - jnp.einsum("ckb,bq->ckq", turned_real, sin_cols, precision=HIGHEST_PRECISION)
        filt_real, filt_imag = filter_spectrum(
            time_part, residue_part, frequency, padded_length, sequence
        )
        prod_real = freq_real * filt_real - freq_imag * filt_imag
        prod_imag = freq_real * filt_imag + freq_imag * filt_real
        back_real = jnp.einsum(
            "ckq,bq->ckb", prod_real, cos_cols, precision=HIGHEST_PRECISION
        ) - jnp.einsum("ckq,bq->ckb", prod_imag, sin_cols, precision=HIGHEST_PRECISION)
        back_imag = jnp.einsum(
            "ckq,bq->ckb", prod_imag, cos_cols, precision=HIGHEST_PRECISION
        ) + jnp.einsum("ckq,bq->ckb", prod_real, sin_cols, precision=HIGHEST_PRECISION)
        spun_real = back_real * cos_turn - back_imag * sin_turn
        spun_imag = back_imag * cos_turn + back_real * sin_turn
        values = jnp.einsum(
            "ka,ckb->cab", cos_rows, spun_real, precision=HIGHEST_PRECISION
        ) - jnp.einsum("ka,ckb->cab", sin_rows, spun_imag, precision=HIGHEST_PRECISION)
        return (values / padded_length).astype(jnp.bfloat16)

    grouped_lines = lines.reshape(group_count, group_size, used_rows, col_count)
    time_groups = decay_time.reshape(group_count, group_size, mode_count)
    residue_groups = residue.reshape(group_count, group_size, mode_count)
    convolved = lax.map(one_group, (grouped_lines, time_groups, residue_groups))
    returned = lax.all_to_all(
        convolved.reshape(1, local_channels, sequence),
        "ctx",
        split_axis=2,
        concat_axis=0,
        tiled=True,
    )
    return jnp.transpose(returned.reshape(channels, length))


def local(activations, norm_gain, short_taps, skip_gain, time_const, residues):
    inputs = activations[0]
    length = inputs.shape[0]
    wide_in = inputs.astype(jnp.float32)
    square_mean = jnp.mean(wide_in * wide_in, axis=-1, keepdims=True)
    normed = (wide_in * lax.rsqrt(square_mean + 1e-06) * norm_gain[0].astype(jnp.float32)).astype(
        jnp.bfloat16
    )
    earlier_rows = from_behind(normed[length - 2 :], "ctx", 1)
    padded = jnp.concatenate([earlier_rows, normed], axis=0)
    wide_taps = short_taps[0].astype(jnp.float32)
    features = []
    for branch in range(3):
        total = jnp.zeros(inputs.shape, jnp.float32)
        for offset in range(3):
            total = total + wide_taps[branch, offset][None, :] * padded[
                2 - offset : 2 - offset + length
            ].astype(jnp.float32)
        features.append(total)
    query_feat, key_feat, value_feat = features
    mixed_in = (key_feat * value_feat).astype(jnp.bfloat16)
    conv_out = spectral_conv(mixed_in, time_const[0], residues[0])
    direct = skip_gain[0].astype(jnp.float32)[None, :] * mixed_in.astype(jnp.float32)
    block_out = (wide_in + query_feat * (conv_out.astype(jnp.float32) + direct)).astype(
        jnp.bfloat16
    )
    return from_behind_2(block_out[None], "phase", 1)


def solution(mesh):
    in_specs = (
        P("phase", "ctx", None),
        P("phase", None),
        P("phase", None, None, None),
        P("phase", None),
        P("phase", "ctx", None),
        P("phase", "ctx", None),
    )
    out_specs = P("phase", "ctx", None)
    return jax.shard_map(local, mesh=mesh, in_specs=in_specs, out_specs=out_specs, check_vma=False)
```

profile of v0, /device:TPU:1, one launch (start us, length us, event | category | flops | bytes accessed | tf_op | source)
XLA Modules:
  0.0 359.3 jit_solution(15073783701809906949)
XLA Ops:
  3.7 4.6 %collective-permute-start = (bf16[2,4096]{1,0:T(2,128)(2,1)S(1)}, bf16[2,4096]{1,0:T(2,128)(2,1)S(1)}, u32[]{:S(2)}, u32[]{:S(2)}) collective-permute-start(bf16[2,4096]{1,0:T(2,128)(2,1)S(1)} %copy.106), channel_id=1, source_target_pairs={{0,1},{1,2},{2,3},{3,4},{4,5},{5,6},{6,7},{7,8},{8,9},{9,10},{10,1... | collective-permute-start | bytes 49160 | tf_op jit(solution)/shard_map/ppermute | solution.py:13
  9.1 3.5 collective-permute-done
  13.1 5.6 %fusion.215 = bf16[128,4096]{0,1:T(8,128)(2,1)} fusion(bf16[128,4096]{0,1:T(8,128)(2,1)S(1)} %fusion.220, f32[4096]{0:T(1024)S(1)} %bitcast.389, f32[4096]{0:T(1024)S(1)} %bitcast.390, f32[4096]{0:T(1024)S(1)} %bitcast.391, f32[4096]{0:T(1024)S(1)} %bitcast.392, f32[4096]{0:T(1024)S(1)} %bitcast.393, f32[4096]{0:T(1024)S(1)} %bitcast.394, ...), kind=kLoop, calls=%fused_computation.400 | loop fusion | flops 11010048 | bytes 2211840 | tf_op jit(solution)/shard_map/convert_element_type | solution.py:141
  18.7 9.2 %all-to-all-start = ((bf16[64,64,128]{2,1,0:T(8,128)(2,1)}), bf16[64,64,128]{2,1,0:T(8,128)(2,1)}, u32[]{:S(2)}, u32[]{:S(2)}) async-start(bf16[64,64,128]{2,1,0:T(8,128)(2,1)} %bitcast.15), calls=%async_computation | async-start | bytes 2097152 | tf_op jit(solution)/shard_map/all_to_all | solution.py:54
  28.2 28.3 %all-to-all-done = bf16[64,64,128]{2,1,0:T(8,128)(2,1)} async-done(((bf16[64,64,128]{2,1,0:T(8,128)(2,1)}), bf16[64,64,128]{2,1,0:T(8,128)(2,1)}, u32[]{:S(2)}, u32[]{:S(2)}) %all-to-all-start) | async-done | bytes 1048608 | tf_op jit(solution)/shard_map/all_to_all | solution.py:54
  56.5 152.4 %while.18 = (s32[]{:T(128)}, bf16[4,16,64,128]{3,2,1,0:T(8,128)(2,1)}, bf16[4,16,64,128]{3,1,0,2:T(8,128)(2,1)}, f32[4,16,16]{1,0,2:T(4,128)S(1)}, f32[4,16,16]{1,0,2:T(4,128)S(1)}, /*index=5*/s32[128]{0:T(128)S(1)}, s32[]{:T(128)}) while((s32[]{:T(128)}, bf16[4,16,64,128]{3,2,1,0:T(8,128)(2,1)}, ...), condition=%wide.region_2.3_spmd.clone.clone.clone, body=%wide.region_1.2_spmd.clone.clone.clone.sunk | while | flops 4104389632 | bytes 44585556 | solution.py:110
  85.6 12.2 %multiply_subtract_fusion.9 = (f32[16,128,128]{2,1,0:T(8,128)S(1)}, f32[16,128,128]{2,1,0:T(8,128)S(1)}, f32[16,128,128]{2,1,0:T(8,128)S(1)}, f32[16,128,128]{2,1,0:T(8,128)S(1)}) fusion(f32[16,128,128]{2,1,0:T(8,128)S(1)} %convolution_add_fusion.4, f32[16]{0:T(128)S(1)} %broadcast_multiply_fusion.32, f32[16]{0:T(128)S(1)} %get-tuple-element.1229, ...), kind=kOutput, calls=%fused_computation.108.clone.1 | convolution fusion | flops 471564288 | bytes 8721408 | tf_op jit(solution)/shard_map/while/body/eval_jaxpr/ckb,bq->ckq/dot_general | solution.py:88
  104.8 2.2 fusion.284
  116.9 12.2 %multiply_subtract_fusion.9 = (f32[16,128,128]{2,1,0:T(8,128)S(1)}, f32[16,128,128]{2,1,0:T(8,128)S(1)}, f32[16,128,128]{2,1,0:T(8,128)S(1)}, f32[16,128,128]{2,1,0:T(8,128)S(1)}) fusion(f32[16,128,128]{2,1,0:T(8,128)S(1)} %convolution_add_fusion.4, f32[16]{0:T(128)S(1)} %broadcast_multiply_fusion.32, f32[16]{0:T(128)S(1)} %get-tuple-element.1229, ...), kind=kOutput, calls=%fused_computation.108.clone.1 | convolution fusion | flops 471564288 | bytes 8721408 | tf_op jit(solution)/shard_map/while/body/eval_jaxpr/ckb,bq->ckq/dot_general | solution.py:88
  136.1 2.2 fusion.284
  148.3 12.2 %multiply_subtract_fusion.9 = (f32[16,128,128]{2,1,0:T(8,128)S(1)}, f32[16,128,128]{2,1,0:T(8,128)S(1)}, f32[16,128,128]{2,1,0:T(8,128)S(1)}, f32[16,128,128]{2,1,0:T(8,128)S(1)}) fusion(f32[16,128,128]{2,1,0:T(8,128)S(1)} %convolution_add_fusion.4, f32[16]{0:T(128)S(1)} %broadcast_multiply_fusion.32, f32[16]{0:T(128)S(1)} %get-tuple-element.1229, ...), kind=kOutput, calls=%fused_computation.108.clone.1 | convolution fusion | flops 471564288 | bytes 8721408 | tf_op jit(solution)/shard_map/while/body/eval_jaxpr/ckb,bq->ckq/dot_general | solution.py:88
  167.5 2.2 fusion.284
  179.6 12.2 %multiply_subtract_fusion.9 = (f32[16,128,128]{2,1,0:T(8,128)S(1)}, f32[16,128,128]{2,1,0:T(8,128)S(1)}, f32[16,128,128]{2,1,0:T(8,128)S(1)}, f32[16,128,128]{2,1,0:T(8,128)S(1)}) fusion(f32[16,128,128]{2,1,0:T(8,128)S(1)} %convolution_add_fusion.4, f32[16]{0:T(128)S(1)} %broadcast_multiply_fusion.32, f32[16]{0:T(128)S(1)} %get-tuple-element.1229, ...), kind=kOutput, calls=%fused_computation.108.clone.1 | convolution fusion | flops 471564288 | bytes 8721408 | tf_op jit(solution)/shard_map/while/body/eval_jaxpr/ckb,bq->ckq/dot_general | solution.py:88
  198.8 2.2 fusion.284
  210.4 6.8 %copy.111 = bf16[1,64,8192]{1,0,2:T(2,128)(2,1)} copy(bf16[1,64,8192]{2,1,0:T(8,128)(2,1)S(1)} %reshape.1431) | data formatting | bytes 2097152 | tf_op jit(solution)/shard_map/reshape | solution.py:112
  217.8 45.2 %reduce = bf16[8192,64]{1,0:T(8,128)(2,1)S(1)} reduce(bf16[8192,1,64]{2,1,0:T(2,128)(2,1)} %bitcast.378, bf16[]{:T(256)} %broadcast.1415), dimensions={1}, to_apply=%bitcast.256.reduce_sub_computation | reduce | bytes 2097154
  263.0 2.3 reshape.1506
  265.3 6.2 %all-to-all-start.1 = ((bf16[64,2,4096]{2,1,0:T(2,128)(2,1)}), bf16[64,2,4096]{2,1,0:T(2,128)(2,1)S(1)}, u32[]{:S(2)}, u32[]{:S(2)}) async-start(bf16[64,2,4096]{2,1,0:T(2,128)(2,1)} %reshape.1506), calls=%async_computation.1 | async-start | bytes 2097152 | tf_op jit(solution)/shard_map/all_to_all | solution.py:111
  271.5 28.5 %all-to-all-done.1 = bf16[64,2,4096]{2,1,0:T(2,128)(2,1)S(1)} async-done(((bf16[64,2,4096]{2,1,0:T(2,128)(2,1)}), bf16[64,2,4096]{2,1,0:T(2,128)(2,1)S(1)}, u32[]{:S(2)}, u32[]{:S(2)}) %all-to-all-start.1) | async-done | bytes 1048608 | tf_op jit(solution)/shard_map/all_to_all | solution.py:111
  300.1 7.0 %reshape.1507 = bf16[8192,1,64]{2,1,0:T(2,128)(2,1)} reshape(bf16[64,2,4096]{2,1,0:T(2,128)(2,1)S(1)} %all-to-all-done.1) | data formatting | bytes 2097152
  307.0 8.2 %copy.112 = bf16[1,64,8192]{2,1,0:T(8,128)(2,1)S(1)} copy(bf16[1,64,8192]{1,0,2:T(2,128)(2,1)} %bitcast.379) | data formatting | bytes 2097152 | tf_op jit(solution)/shard_map/all_to_all | solution.py:111
  317.6 6.1 %fusion.221 = bf16[128,4096]{0,1:T(8,128)(2,1)S(1)} fusion(bf16[128,4096]{0,1:T(8,128)(2,1)S(1)} %copy-done.3, f32[64,1,64,128]{3,2,0,1:T(8,128)S(1)} %copy.113, bf16[128,4096]{0,1:T(8,128)(2,1)} %fusion.215, bf16[1,128,4096]{1,2,0:T(8,128)(2,1)S(1)} %copy-done.1, f32[4096]{0:T(1024)S(1)} %bitcast.395, f32[4096]{0:T(1024)S(1)} %bitcast.387, ...), kind=kLoop, calls=%fused_computation.406 | loop fusion | flops 11010048 | bytes 6373376 | tf_op jit(solution)/shard_map/convert_element_type | solution.py:144
  323.7 4.0 %collective-permute-start.1 = (bf16[1,128,4096]{1,2,0:T(8,128)(2,1)S(1)}, bf16[1,128,4096]{1,2,0:T(8,128)(2,1)S(1)}, u32[]{:S(2)}, u32[]{:S(2)}) collective-permute-start(bf16[1,128,4096]{1,2,0:T(8,128)(2,1)S(1)} %bitcast.381), channel_id=1, source_target_pairs={{448,0},{0,64},{64,128},{128,192},{192,256},{256,320},{320,384},{3... | collective-permute-start | bytes 3145736 | tf_op jit(solution)/shard_map/ppermute | solution.py:19
  327.7 30.1 %collective-permute-done.1 = bf16[1,128,4096]{1,2,0:T(8,128)(2,1)S(1)} collective-permute-done((bf16[1,128,4096]{1,2,0:T(8,128)(2,1)S(1)}, bf16[1,128,4096]{1,2,0:T(8,128)(2,1)S(1)}, u32[]{:S(2)}, u32[]{:S(2)}) %collective-permute-start.1) | collective-permute-done | bytes 1048608 | tf_op jit(solution)/shard_map/ppermute | solution.py:19
  (249 shorter events, 77.2 us)
Async XLA Ops:
  0.0 2.2 copy-start.10
  1.6 1.7 copy-start
  3.0 10.1 %copy-start.2 = (bf16[128,4096]{0,1:T(8,128)(2,1)}, bf16[128,4096]{0,1:T(8,128)(2,1)S(1)}, u32[]{:S(2)}) copy-start(bf16[128,4096]{0,1:T(8,128)(2,1)S(1)} %fusion.220) | copy-start | bytes 3145732
  3.0 5.4 %copy-start.6 = (bf16[1,3,3,4096]{3,2,1,0:T(4,128)(2,1)S(1)}, bf16[1,3,3,4096]{3,2,1,0:T(4,128)(2,1)}, u32[]{:S(2)}) copy-start(bf16[1,3,3,4096]{3,2,1,0:T(4,128)(2,1)} %param.10) | copy-start | bytes 221188
  3.7 8.8 %collective-permute-start = (bf16[2,4096]{1,0:T(2,128)(2,1)S(1)}, bf16[2,4096]{1,0:T(2,128)(2,1)S(1)}, u32[]{:S(2)}, u32[]{:S(2)}) collective-permute-start(bf16[2,4096]{1,0:T(2,128)(2,1)S(1)} %copy.106), channel_id=1, source_target_pairs={{0,1},{1,2},{2,3},{3,4},{4,5},{5,6},{6,7},{7,8},{8,9},{9,10},{10,1... | collective-permute-start | bytes 49160 | tf_op jit(solution)/shard_map/ppermute | solution.py:13
  13.1 5.7 %copy-start.4 = (bf16[2,4096]{0,1:T(8,128)(2,1)}, bf16[2,4096]{0,1:T(8,128)(2,1)S(1)}, u32[]{:S(2)}) copy-start(bf16[2,4096]{0,1:T(8,128)(2,1)S(1)} %copy.107) | copy-start | bytes 49156
  13.1 14.9 %copy-start.12 = (f32[1,64,16]{1,2,0:T(8,128)S(1)}, f32[1,64,16]{1,2,0:T(8,128)}, u32[]{:S(2)}) copy-start(f32[1,64,16]{1,2,0:T(8,128)} %param.13) | copy-start | bytes 12292
  13.1 15.0 %copy-start.13 = (f32[1,64,16]{1,2,0:T(8,128)S(1)}, f32[1,64,16]{1,2,0:T(8,128)}, u32[]{:S(2)}) copy-start(f32[1,64,16]{1,2,0:T(8,128)} %param.12) | copy-start | bytes 12292
  18.7 37.7 %all-to-all-start = ((bf16[64,64,128]{2,1,0:T(8,128)(2,1)}), bf16[64,64,128]{2,1,0:T(8,128)(2,1)}, u32[]{:S(2)}, u32[]{:S(2)}) async-start(bf16[64,64,128]{2,1,0:T(8,128)(2,1)} %bitcast.15), calls=%async_computation | async-start | bytes 2097152 | tf_op jit(solution)/shard_map/all_to_all | solution.py:54
  263.0 8.5 %copy-start.11 = (bf16[1,4096]{1,0:T(2,128)(2,1)S(1)}, bf16[1,4096]{1,0:T(2,128)(2,1)}, u32[]{:S(2)}) copy-start(bf16[1,4096]{1,0:T(2,128)(2,1)} %param.11) | copy-start | bytes 24580
  265.3 34.8 %all-to-all-start.1 = ((bf16[64,2,4096]{2,1,0:T(2,128)(2,1)}), bf16[64,2,4096]{2,1,0:T(2,128)(2,1)S(1)}, u32[]{:S(2)}, u32[]{:S(2)}) async-start(bf16[64,2,4096]{2,1,0:T(2,128)(2,1)} %reshape.1506), calls=%async_computation.1 | async-start | bytes 2097152 | tf_op jit(solution)/shard_map/all_to_all | solution.py:111
  315.7 1.3 copy-start.1
  315.8 1.5 copy-start.3
  315.8 1.8 copy-start.5
  315.8 1.8 copy-start.7
  315.8 1.8 copy-start.8
  315.8 1.8 copy-start.9
  323.7 34.1 %collective-permute-start.1 = (bf16[1,128,4096]{1,2,0:T(8,128)(2,1)S(1)}, bf16[1,128,4096]{1,2,0:T(8,128)(2,1)S(1)}, u32[]{:S(2)}, u32[]{:S(2)}) collective-permute-start(bf16[1,128,4096]{1,2,0:T(8,128)(2,1)S(1)} %bitcast.381), channel_id=1, source_target_pairs={{448,0},{0,64},{64,128},{128,192},{192,256},{256,320},{320,384},{3... | collective-permute-start | bytes 3145736 | tf_op jit(solution)/shard_map/ppermute | solution.py:19
where the time goes:
time: 363 us; the launch traced here: 359 us
  matrix products  114 us (31%)
  waiting for transfers between devices  90.3 us (25%)
  other arithmetic  64.3 us (18%)
  local copies, waits for them, and re-layouts  37.6 us (10%)
  loops' own time  28.4 us (8%)
  starting transfers between devices  24.1 us (7%)
    dot_general x4, matrix products, one_group(): jnp.einsum('ckb,bq->ckq', turned_real, sin_cols, precision=HIGHEST_PRECIS...  48.8 us
    unnamed x2, other arithmetic  45.3 us
    ppermute x1, waiting for transfers between devices, from_behind_2(): return lax.ppermute(block, axis, route)  30.1 us
    all_to_all x1, waiting for transfers between devices, spectral_conv(): lax.all_to_all(convolved.reshape(1, local_channels, sequence), 'ctx', spl...  28.5 us
    another operation x1, loops' own time, spectral_conv(): convolved = lax.map(one_group, (grouped_lines, time_groups, residue_groups))  28.4 us
    all_to_all x1, waiting for transfers between devices, spectral_conv(): lax.all_to_all(pieces, 'ctx', split_axis=0, concat_axis=2, tiled=True)[0]  28.3 us
    unnamed x33, local copies, waits for them, and re-layouts  12.4 us
    all_to_all x1, starting transfers between devices, spectral_conv(): lax.all_to_all(pieces, 'ctx', split_axis=0, concat_axis=2, tiled=True)[0]  9.25 us
  transfers between devices with their start and end apart: 4, of which 4 were waited for; matrix products, arithmetic and copies ran while one was open for 0% of the time, Pallas kernels for 0%

commit v1 on v0

--- a/solution.py
+++ b/solution.py
@@ -108,12 +108,18 @@
     time_groups = decay_time.reshape(group_count, group_size, mode_count)
     residue_groups = residue.reshape(group_count, group_size, mode_count)
     convolved = lax.map(one_group, (grouped_lines, time_groups, residue_groups))
-    returned = lax.all_to_all(
-        convolved.reshape(1, local_channels, sequence),
-        "ctx",
-        split_axis=2,
-        concat_axis=0,
-        tiled=True,
+    returned = jnp.concatenate(
+        lax.all_to_all(
+            jnp.stack(
+                jnp.split(
+                    convolved.reshape(1, local_channels, sequence), lax.axis_size("ctx"), axis=2
+                )
+            ),
+            "ctx",
+            0,
+            0,
+        ),
+        axis=0,
     )
     return jnp.transpose(returned.reshape(channels, length))
 

time: 363 us -> 297 us (0.82)
  other arithmetic: 64.3 us -> 19 us
  loops' own time: 28.4 us -> 1.94 us
  local copies, waits for them, and re-layouts: 37.6 us -> 44.7 us
    unnamed x2 -> x0, other arithmetic: 45.3 us -> none
    unnamed x33 -> x92, local copies, waits for them, and re-layouts: 12.4 us -> 39.9 us
    another operation x1, loops' own time: 28.4 us -> 1.94 us  [spectral_conv(): convolved = lax.map(one_group, (grouped_lines, time_groups, residue_groups))]
    all_to_all x1 -> x0, local copies, waits for them, and re-layouts: 8.16 us -> none  [spectral_conv(): lax.all_to_all(convolved.reshape(1, local_channels, sequence), 'ctx', spl...]
    reshape x2 -> x1, local copies, waits for them, and re-layouts: 8.35 us -> 0.49 us  [spectral_conv(): convolved.reshape(1, local_channels, sequence)]
    dynamic_slice x8, local copies, waits for them, and re-layouts: 3.99 us -> 0.25 us  [spectral_conv(): convolved = lax.map(one_group, (grouped_lines, time_groups, residue_groups))]
where the time goes in v1:
time: 297 us; the launch traced here: 293 us
  matrix products  112 us (38%)
  waiting for transfers between devices  90.3 us (30%)
  local copies, waits for them, and re-layouts  44.7 us (15%)
  starting transfers between devices  24.4 us (8%)
  other arithmetic  19 us (6%)
    dot_general x4, matrix products, one_group(): jnp.einsum('ckb,bq->ckq', turned_real, sin_cols, precision=HIGHEST_PRECIS...  48.9 us
    unnamed x92, local copies, waits for them, and re-layouts  39.9 us
    ppermute x1, waiting for transfers between devices, from_behind_2(): return lax.ppermute(block, axis, route)  30.1 us
    all_to_all x1, waiting for transfers between devices, spectral_conv(): lax.all_to_all(jnp.stack(jnp.split(convolved.reshape(1, local_channels, s...  28.4 us
    all_to_all x1, waiting for transfers between devices, spectral_conv(): lax.all_to_all(pieces, 'ctx', split_axis=0, concat_axis=2, tiled=True)[0]  28.3 us
    all_to_all x1, starting transfers between devices, spectral_conv(): lax.all_to_all(pieces, 'ctx', split_axis=0, concat_axis=2, tiled=True)[0]  9.19 us
    dot_general x4, matrix products, one_group(): jnp.einsum('ckb,bq->ckq', turned_imag, sin_cols, precision=HIGHEST_PRECIS...  8.12 us
    dot_general x4, matrix products, one_group(): jnp.einsum('ckb,bq->ckq', turned_imag, cos_cols, precision=HIGHEST_PRECIS...  8.08 us
  transfers between devices with their start and end apart: 4, of which 4 were waited for; matrix products, arithmetic and copies ran while one was open for 0% of the time, Pallas kernels for 0%

profile of v1, /device:TPU:1, one launch (start us, length us, event | category | flops | bytes accessed | tf_op | source)
XLA Modules:
  0.0 293.1 jit_solution(16925029185464831906)
XLA Ops:
  3.9 4.6 %collective-permute-start = (bf16[2,4096]{1,0:T(2,128)(2,1)S(1)}, bf16[2,4096]{1,0:T(2,128)(2,1)S(1)}, u32[]{:S(2)}, u32[]{:S(2)}) collective-permute-start(bf16[2,4096]{1,0:T(2,128)(2,1)S(1)} %copy.108), channel_id=1, source_target_pairs={{0,1},{1,2},{2,3},{3,4},{4,5},{5,6},{6,7},{7,8},{8,9},{9,10},{10,1... | collective-permute-start | bytes 49160 | tf_op jit(solution)/shard_map/ppermute | solution.py:13
  9.2 3.5 %collective-permute-done = bf16[2,4096]{1,0:T(2,128)(2,1)S(1)} collective-permute-done((bf16[2,4096]{1,0:T(2,128)(2,1)S(1)}, bf16[2,4096]{1,0:T(2,128)(2,1)S(1)}, u32[]{:S(2)}, u32[]{:S(2)}) %collective-permute-start) | collective-permute-done | bytes 16416 | tf_op jit(solution)/shard_map/ppermute | solution.py:13
  13.2 5.6 %fusion.215 = bf16[128,4096]{0,1:T(8,128)(2,1)} fusion(bf16[128,4096]{0,1:T(8,128)(2,1)S(1)} %fusion.220, f32[4096]{0:T(1024)S(1)} %bitcast.636, f32[4096]{0:T(1024)S(1)} %bitcast.637, f32[4096]{0:T(1024)S(1)} %bitcast.638, f32[4096]{0:T(1024)S(1)} %bitcast.639, f32[4096]{0:T(1024)S(1)} %bitcast.640, f32[4096]{0:T(1024)S(1)} %bitcast.641, ...), kind=kLoop, calls=%fused_computation.400 | loop fusion | flops 11010048 | bytes 2211840 | tf_op jit(solution)/shard_map/convert_element_type | solution.py:147
  18.8 9.2 %all-to-all-start = ((bf16[64,64,128]{2,1,0:T(8,128)(2,1)}), bf16[64,64,128]{2,1,0:T(8,128)(2,1)S(1)}, u32[]{:S(2)}, u32[]{:S(2)}) async-start(bf16[64,64,128]{2,1,0:T(8,128)(2,1)} %bitcast.15), calls=%async_computation | async-start | bytes 2097152 | tf_op jit(solution)/shard_map/all_to_all | solution.py:54
  28.2 28.3 %all-to-all-done = bf16[64,64,128]{2,1,0:T(8,128)(2,1)S(1)} async-done(((bf16[64,64,128]{2,1,0:T(8,128)(2,1)}), bf16[64,64,128]{2,1,0:T(8,128)(2,1)S(1)}, u32[]{:S(2)}, u32[]{:S(2)}) %all-to-all-start) | async-done | bytes 1048608 | tf_op jit(solution)/shard_map/all_to_all | solution.py:54
  56.6 120.3 %while.18 = (s32[]{:T(128)}, bf16[4,16,64,128]{3,2,1,0:T(8,128)(2,1)S(1)}, bf16[4,16,64,128]{3,1,0,2:T(8,128)(2,1)S(1)}, f32[4,16,16]{1,0,2:T(4,128)S(1)}, f32[4...) while((s32[]{:T(128)}, bf16[4,16,64,128]{3,2,1,0:T(8,128)(2,1)S(1)}, ...), condition=%wide.region_2.3_spmd.clone.clone.clone, body=%wide.region_1.2_spmd.clone.clone.clone.sunk | while | flops 4104389632 | bytes 44585048 | solution.py:110
  58.8 2.0 fusion.277
  60.8 2.0 convolution_add_fusion.4
  63.4 2.0 fusion.281
  66.0 12.2 %multiply_subtract_fusion.9 = (f32[16,128,128]{2,1,0:T(8,128)S(1)}, f32[16,128,128]{2,1,0:T(8,128)S(1)}, f32[16,128,128]{2,1,0:T(8,128)S(1)}, f32[16,128,128]{2,1,0:T(8,128)S(1)}) fusion(f32[16,128,128]{2,1,0:T(8,128)S(1)} %convolution_add_fusion.4, f32[16]{0:T(128)S(1)} %broadcast_multiply_fusion.32, f32[16]{0:T(128)S(1)} %get-tuple-element.1211, ...), kind=kOutput, calls=%fused_computation.108.clone.1 | convolution fusion | flops 471564288 | bytes 8721408 | tf_op jit(solution)/shard_map/while/body/eval_jaxpr/ckb,bq->ckq/dot_general | solution.py:88
  88.7 2.0 fusion.277
  90.8 2.0 convolution_add_fusion.4
  93.3 2.0 fusion.281
  95.9 12.2 %multiply_subtract_fusion.9 = (f32[16,128,128]{2,1,0:T(8,128)S(1)}, f32[16,128,128]{2,1,0:T(8,128)S(1)}, f32[16,128,128]{2,1,0:T(8,128)S(1)}, f32[16,128,128]{2,1,0:T(8,128)S(1)}) fusion(f32[16,128,128]{2,1,0:T(8,128)S(1)} %convolution_add_fusion.4, f32[16]{0:T(128)S(1)} %broadcast_multiply_fusion.32, f32[16]{0:T(128)S(1)} %get-tuple-element.1211, ...), kind=kOutput, calls=%fused_computation.108.clone.1 | convolution fusion | flops 471564288 | bytes 8721408 | tf_op jit(solution)/shard_map/while/body/eval_jaxpr/ckb,bq->ckq/dot_general | solution.py:88
  120.7 2.0 convolution_add_fusion.4
  123.2 2.0 fusion.281
  125.9 12.2 %multiply_subtract_fusion.9 = (f32[16,128,128]{2,1,0:T(8,128)S(1)}, f32[16,128,128]{2,1,0:T(8,128)S(1)}, f32[16,128,128]{2,1,0:T(8,128)S(1)}, f32[16,128,128]{2,1,0:T(8,128)S(1)}) fusion(f32[16,128,128]{2,1,0:T(8,128)S(1)} %convolution_add_fusion.4, f32[16]{0:T(128)S(1)} %broadcast_multiply_fusion.32, f32[16]{0:T(128)S(1)} %get-tuple-element.1211, ...), kind=kOutput, calls=%fused_computation.108.clone.1 | convolution fusion | flops 471564288 | bytes 8721408 | tf_op jit(solution)/shard_map/while/body/eval_jaxpr/ckb,bq->ckq/dot_general | solution.py:88
  150.6 2.0 convolution_add_fusion.4
  155.8 12.2 %multiply_subtract_fusion.9 = (f32[16,128,128]{2,1,0:T(8,128)S(1)}, f32[16,128,128]{2,1,0:T(8,128)S(1)}, f32[16,128,128]{2,1,0:T(8,128)S(1)}, f32[16,128,128]{2,1,0:T(8,128)S(1)}) fusion(f32[16,128,128]{2,1,0:T(8,128)S(1)} %convolution_add_fusion.4, f32[16]{0:T(128)S(1)} %broadcast_multiply_fusion.32, f32[16]{0:T(128)S(1)} %get-tuple-element.1211, ...), kind=kOutput, calls=%fused_computation.108.clone.1 | convolution fusion | flops 471564288 | bytes 8721408 | tf_op jit(solution)/shard_map/while/body/eval_jaxpr/ckb,bq->ckq/dot_general | solution.py:88
  216.1 6.5 %all-to-all-start.1 = ((bf16[64,1,64,128]{3,2,1,0:T(8,128)(2,1)}), bf16[64,1,64,128]{3,2,1,0:T(8,128)(2,1)}, u32[]{:S(2)}, u32[]{:S(2)}) async-start(bf16[64,1,64,128]{3,2,1,0:T(8,128)(2,1)} %constant_dynamic-update-slice_fusion), calls=%async_computation.1 | async-start | bytes 2097152 | tf_op jit(solution)/shard_map/all_to_all | solution.py:112
  222.7 28.4 %all-to-all-done.1 = bf16[64,1,64,128]{3,2,1,0:T(8,128)(2,1)} async-done(((bf16[64,1,64,128]{3,2,1,0:T(8,128)(2,1)}), bf16[64,1,64,128]{3,2,1,0:T(8,128)(2,1)}, u32[]{:S(2)}, u32[]{:S(2)}) %all-to-all-start.1) | async-done | bytes 1048608 | tf_op jit(solution)/shard_map/all_to_all | solution.py:112
  251.2 6.3 %fusion.221 = bf16[128,4096]{0,1:T(8,128)(2,1)S(1)} fusion(bf16[128,4096]{0,1:T(8,128)(2,1)S(1)} %copy-done.3, bf16[128,4096]{0,1:T(8,128)(2,1)} %fusion.215, bf16[64,1,64,128]{3,2,1,0:T(8,128)(2,1)} %all-to-all-done.1, bf16[1,128,4096]{1,2,0:T(8,128)(2,1)S(1)} %copy-done.1, f32[4096]{0:T(1024)S(1)} %bitcast.642, f32[4096]{0:T(1024)S(1)} %bitcast.634, ...), kind=kLoop, calls=%fused_computation.406 | loop fusion | flops 11534336 | bytes 5324800 | tf_op jit(solution)/shard_map/convert_element_type | solution.py:150
  257.5 4.0 %collective-permute-start.1 = (bf16[1,128,4096]{1,2,0:T(8,128)(2,1)S(1)}, bf16[1,128,4096]{1,2,0:T(8,128)(2,1)S(1)}, u32[]{:S(2)}, u32[]{:S(2)}) collective-permute-start(bf16[1,128,4096]{1,2,0:T(8,128)(2,1)S(1)} %bitcast.628), channel_id=1, source_target_pairs={{448,0},{0,64},{64,128},{128,192},{192,256},{256,320},{320,384},{3... | collective-permute-start | bytes 3145736 | tf_op jit(solution)/shard_map/ppermute | solution.py:19
  261.5 30.1 %collective-permute-done.1 = bf16[1,128,4096]{1,2,0:T(8,128)(2,1)S(1)} collective-permute-done((bf16[1,128,4096]{1,2,0:T(8,128)(2,1)S(1)}, bf16[1,128,4096]{1,2,0:T(8,128)(2,1)S(1)}, u32[]{:S(2)}, u32[]{:S(2)}) %collective-permute-start.1) | collective-permute-done | bytes 1048608 | tf_op jit(solution)/shard_map/ppermute | solution.py:19
  (304 shorter events, 97.0 us)
Async XLA Ops:
  1.6 1.5 copy-start
  1.6 0.7 copy-start.10
  3.1 10.1 %copy-start.2 = (bf16[128,4096]{0,1:T(8,128)(2,1)}, bf16[128,4096]{0,1:T(8,128)(2,1)S(1)}, u32[]{:S(2)}) copy-start(bf16[128,4096]{0,1:T(8,128)(2,1)S(1)} %fusion.220) | copy-start | bytes 3145732
  3.5 5.0 %copy-start.6 = (bf16[1,3,3,4096]{3,2,1,0:T(4,128)(2,1)S(1)}, bf16[1,3,3,4096]{3,2,1,0:T(4,128)(2,1)}, u32[]{:S(2)}) copy-start(bf16[1,3,3,4096]{3,2,1,0:T(4,128)(2,1)} %param.10) | copy-start | bytes 221188
  3.9 8.8 %collective-permute-start = (bf16[2,4096]{1,0:T(2,128)(2,1)S(1)}, bf16[2,4096]{1,0:T(2,128)(2,1)S(1)}, u32[]{:S(2)}, u32[]{:S(2)}) collective-permute-start(bf16[2,4096]{1,0:T(2,128)(2,1)S(1)} %copy.108), channel_id=1, source_target_pairs={{0,1},{1,2},{2,3},{3,4},{4,5},{5,6},{6,7},{7,8},{8,9},{9,10},{10,1... | collective-permute-start | bytes 49160 | tf_op jit(solution)/shard_map/ppermute | solution.py:13
  13.2 5.6 %copy-start.4 = (bf16[2,4096]{0,1:T(8,128)(2,1)}, bf16[2,4096]{0,1:T(8,128)(2,1)S(1)}, u32[]{:S(2)}) copy-start(bf16[2,4096]{0,1:T(8,128)(2,1)S(1)} %copy.109) | copy-start | bytes 49156
  18.8 9.2 %copy-start.12 = (f32[1,64,16]{1,2,0:T(8,128)S(1)}, f32[1,64,16]{1,2,0:T(8,128)}, u32[]{:S(2)}) copy-start(f32[1,64,16]{1,2,0:T(8,128)} %param.13) | copy-start | bytes 12292
  18.8 9.3 %copy-start.13 = (f32[1,64,16]{1,2,0:T(8,128)S(1)}, f32[1,64,16]{1,2,0:T(8,128)}, u32[]{:S(2)}) copy-start(f32[1,64,16]{1,2,0:T(8,128)} %param.12) | copy-start | bytes 12292
  18.8 37.8 %all-to-all-start = ((bf16[64,64,128]{2,1,0:T(8,128)(2,1)}), bf16[64,64,128]{2,1,0:T(8,128)(2,1)S(1)}, u32[]{:S(2)}, u32[]{:S(2)}) async-start(bf16[64,64,128]{2,1,0:T(8,128)(2,1)} %bitcast.15), calls=%async_computation | async-start | bytes 2097152 | tf_op jit(solution)/shard_map/all_to_all | solution.py:54
  195.5 27.1 %copy-start.11 = (bf16[1,4096]{1,0:T(2,128)(2,1)S(1)}, bf16[1,4096]{1,0:T(2,128)(2,1)}, u32[]{:S(2)}) copy-start(bf16[1,4096]{1,0:T(2,128)(2,1)} %param.11) | copy-start | bytes 24580
  195.5 55.6 %copy-start.9 = (f32[1,1,4096]{2,1,0:T(1,128)S(1)}, f32[1,1,4096]{2,1,0:T(1,128)}, u32[]{:S(2)}) copy-start(f32[1,1,4096]{2,1,0:T(1,128)} %get-tuple-element.1078) | copy-start | bytes 49156
  196.7 54.4 %copy-start.5 = (bf16[2,4096]{0,1:T(8,128)(2,1)S(1)}, bf16[2,4096]{0,1:T(8,128)(2,1)}, u32[]{:S(2)}) copy-start(bf16[2,4096]{0,1:T(8,128)(2,1)} %copy-done.4) | copy-start | bytes 49156
  216.1 35.0 %copy-start.1 = (bf16[1,128,4096]{1,2,0:T(8,128)(2,1)S(1)}, bf16[1,128,4096]{1,2,0:T(8,128)(2,1)}, u32[]{:S(2)}) copy-start(bf16[1,128,4096]{1,2,0:T(8,128)(2,1)} %copy-done) | copy-start | bytes 3145732
  216.1 35.0 %copy-start.3 = (bf16[128,4096]{0,1:T(8,128)(2,1)S(1)}, bf16[128,4096]{0,1:T(8,128)(2,1)}, u32[]{:S(2)}) copy-start(bf16[128,4096]{0,1:T(8,128)(2,1)} %copy-done.2) | copy-start | bytes 3145732
  216.1 35.0 %copy-start.7 = (f32[1,1,4096]{2,1,0:T(1,128)S(1)}, f32[1,1,4096]{2,1,0:T(1,128)}, u32[]{:S(2)}) copy-start(f32[1,1,4096]{2,1,0:T(1,128)} %get-tuple-element.1070) | copy-start | bytes 49156
  216.1 35.0 %copy-start.8 = (f32[1,1,4096]{2,1,0:T(1,128)S(1)}, f32[1,1,4096]{2,1,0:T(1,128)}, u32[]{:S(2)}) copy-start(f32[1,1,4096]{2,1,0:T(1,128)} %get-tuple-element.1077) | copy-start | bytes 49156
  216.1 35.0 %all-to-all-start.1 = ((bf16[64,1,64,128]{3,2,1,0:T(8,128)(2,1)}), bf16[64,1,64,128]{3,2,1,0:T(8,128)(2,1)}, u32[]{:S(2)}, u32[]{:S(2)}) async-start(bf16[64,1,64,128]{3,2,1,0:T(8,128)(2,1)} %constant_dynamic-update-slice_fusion), calls=%async_computation.1 | async-start | bytes 2097152 | tf_op jit(solution)/shard_map/all_to_all | solution.py:112
  257.5 34.1 %collective-permute-start.1 = (bf16[1,128,4096]{1,2,0:T(8,128)(2,1)S(1)}, bf16[1,128,4096]{1,2,0:T(8,128)(2,1)S(1)}, u32[]{:S(2)}, u32[]{:S(2)}) collective-permute-start(bf16[1,128,4096]{1,2,0:T(8,128)(2,1)S(1)} %bitcast.628), channel_id=1, source_target_pairs={{448,0},{0,64},{64,128},{128,192},{192,256},{256,320},{320,384},{3... | collective-permute-start | bytes 3145736 | tf_op jit(solution)/shard_map/ppermute | solution.py:19
